TPU v7x, 32 devices: a whole 2x2x4 slice. The times are simulated.
32 devices in a mesh: row: 16 (over z, y, core), loop: 2 (over x).
Axes of the slice: x: 2, y: 2, z: 4, core: 2. Of those that a mesh axis runs over, the one named last changes fastest.
Arguments:
- panels: float32 [512, 256], P('loop'), may hold values from -0.3 to 0.3
- right_side: float32 [32768, 256], P(('row', 'loop')), may hold values from -6 to 6
- block_users: int32 [768], P(('row', 'loop')), may hold values from 0 to 7
- block_items: int32 [768], P(('row', 'loop')), may hold values from 0 to 1
- masks: int32 [768, 128, 128], P(('row', 'loop')), may hold values 0 or 1
- self_tiles: float32 [32768, 128], P(('row', 'loop')), may hold values from 0 to 0.02
- next_tiles: float32 [32768, 128], P(('row', 'loop')), may hold values from 0 to 0.02
Outputs:
- solution_field: float32 [32768, 256], P(('row', 'loop'))
- residual: float32 [32768, 256], P(('row', 'loop'))
All inputs are finite; a program needn't handle non-finite values. No bound on the sum of `masks` on one device may be relied on, other than what follows from the above.
Results may differ from a plain program's by a relative error of at most 0.00045.
Values sent between devices are 32-bit elements; how exact they have to be, the bound alone decides.
A program may use at most 64 MiB of HBM per device.

v0:
```python
import jax
import jax.numpy as jnp
from jax import lax
from jax.sharding import PartitionSpec as P

ITERS = 2


ridge_weight = 0.5
highest = lax.Precision.HIGHEST


def from_behind(x, axis, by):
    size = lax.axis_size(axis)
    return lax.ppermute(x, axis, [(i, (i + by) % size) for i in range(size)])


def from_behind_2(value, axis, steps):
    count = lax.axis_size(axis)
    initial, last = (max(0, -steps), min(count, count - steps))
    return lax.ppermute(value, axis, [(source, source + steps) for source in range(initial, last)])


def global_sum(values):
    return lax.psum(jnp.sum(values), ("row", "loop"))


def body(panels, right_side, block_users, block_items, masks, self_tiles, next_tiles):
    tile = masks.shape[1]
    width_k = panels.shape[1]
    user_blocks = right_side.shape[0] // tile
    loop_size = lax.axis_size("loop")
    position = lax.axis_index("loop")
    per_panel = block_users.shape[0] // loop_size
    user_ids = jnp.arange(user_blocks, dtype=jnp.int32)
    own_tiles = self_tiles.reshape(user_blocks, tile, tile)
    symmetric = 0.5 * (own_tiles + jnp.swapaxes(own_tiles, 1, 2))
    onward = next_tiles.reshape(user_blocks, tile, tile)
    last_columns = jnp.sum(onward[-1], axis=0)
    inner_columns = jnp.sum(onward[:-1], axis=1)
    degree_base = jnp.sum(symmetric, axis=2) + jnp.sum(onward, axis=2)
    solution_field = jnp.zeros_like(right_side)
    residual = right_side
    direction = right_side
    norm_now = global_sum(residual * residual)
    for turn_index in range(ITERS):
        blocks = direction.reshape(user_blocks, tile, width_k)
        outgoing = jnp.dot(onward[-1].T, blocks[-1], precision=highest)
        carried, carried_columns = from_behind_2((outgoing, last_columns), ("row", "loop"), 1)
        lower_rows = from_behind_2(blocks[0], ("row", "loop"), -1)
        following = jnp.concatenate([blocks[1:], lower_rows[None]], axis=0)
        backward = jnp.einsum("bji,bjk->bik", onward[:-1], blocks[:-1], precision=highest)
        preceding = jnp.concatenate([carried[None], backward], axis=0)
        coupled = jnp.einsum("bij,bjk->bik", symmetric, blocks, precision=highest)
        coupled = (
            coupled + jnp.einsum("bij,bjk->bik", onward, following, precision=highest) + preceding
        )
        degree = degree_base + jnp.concatenate([carried_columns[None], inner_columns], axis=0)
        operate_degree = degree.reshape(-1)
        operate_coupled = coupled.reshape(-1, width_k)
        user_tiles = direction.reshape(user_blocks, tile, width_k)

        def panel_term(held_panel, panel_index):
            first_row = panel_index * per_panel
            chosen_users = lax.dynamic_slice_in_dim(block_users, first_row, per_panel, 0)
            chosen_items = lax.dynamic_slice_in_dim(block_items, first_row, per_panel, 0)
            chosen_masks = lax.dynamic_slice_in_dim(masks, first_row, per_panel, 0).astype(
                jnp.float32
            )
            left_tiles = user_tiles[chosen_users]
            right_tiles = held_panel.reshape(-1, tile, width_k)[chosen_items]
            scores = (
                jnp.einsum("bik,bjk->bij", left_tiles, right_tiles, precision=highest)
                * chosen_masks
            )
            contrib = jnp.einsum("bij,bjk->bik", scores, right_tiles, precision=highest)
            selector = (chosen_users[:, None] == user_ids[None, :]).astype(jnp.float32)
            return jnp.einsum("bn,bik->nik", selector, contrib, precision=highest)

        zero_sum = jnp.zeros_like(user_tiles)

        def visit_turn(turn_index, state):
            summed, held_panel = state
            summed = summed + panel_term(held_panel, (position - turn_index) % loop_size)
            held_panel = from_behind(held_panel, "loop", 1)
            return (summed, held_panel)

        summed, held_panel = lax.fori_loop(0, loop_size - 1, visit_turn, (zero_sum, panels))
        summed = summed + panel_term(held_panel, (position - loop_size + 1) % loop_size)
        gram_part = summed.reshape(-1, width_k)
        image = gram_part + (ridge_weight + operate_degree)[:, None] * direction - operate_coupled
        step_size = norm_now / global_sum(direction * image)
        solution_field = solution_field + step_size * direction
        residual = residual - step_size * image
        norm_next = global_sum(residual * residual)
        direction = residual + norm_next / norm_now * direction
        norm_now = norm_next
    return (solution_field, residual)


def solution(mesh):
    placed = (
        P("loop", None),
        P(("row", "loop"), None),
        P(("row", "loop")),
        P(("row", "loop")),
        P(("row", "loop"), None, None),
        P(("row", "loop"), None),
        P(("row", "loop"), None),
    )
    return jax.shard_map(
        body,
        mesh=mesh,
        in_specs=placed,
        out_specs=(P(("row", "loop"), None), P(("row", "loop"), None)),
        check_vma=False,
    )
```

profile of v0, /device:TPU:0, one launch (start us, length us, event | category | flops | bytes accessed | tf_op | source)
XLA Modules:
  0.0 212.7 jit_solution(18276169605393874482)
XLA Ops:
  0.6 3.0 %collective-permute-start = (f32[256,256]{1,0:T(8,128)}, f32[256,256]{1,0:T(8,128)S(1)}, u32[]{:S(2)}, u32[]{:S(2)}) collective-permute-start(f32[256,256]{1,0:T(8,128)} %param.7), channel_id=1, source_target_pairs={{0,1},{1,0},{2,3},{3,2},{4,5},{5,4},{6,7},{7,6},{8,9},{9,8},{10,11... | collective-permute-start | bytes 786440 | tf_op jit(solution)/shard_map/while/body/eval_jaxpr/ppermute | solution.py:15
  3.6 1.6 slice.59
  5.2 1.3 collective-permute-start.2
  6.5 1.9 fusion.26
  8.4 5.2 %collective-permute-start.3 = (f32[128,256]{1,0:T(8,128)}, f32[128,256]{1,0:T(8,128)}, u32[]{:S(2)}, u32[]{:S(2)}) collective-permute-start(f32[128,256]{1,0:T(8,128)} %fusion.26), channel_id=1, source_target_pairs={{0,1},{1,2},{2,3},{3,4},{4,5},{5,6},{6,7},{7,8},{8,9},{9,10},{10,1... | collective-permute-start | bytes 393224 | tf_op jit(solution)/shard_map/ppermute | solution.py:21
  13.6 0.9 slice_reduce_fusion
  14.5 1.3 collective-permute-start.1
  15.8 1.8 slice.55
  17.6 1.4 fusion.50
  19.0 0.6 compare_select_fusion.2
  20.1 2.0 fusion.46
  22.1 1.8 gather_fusion
  23.9 0.6 gather_fusion.1
  24.6 3.8 %convolution_multiply_fusion.3 = f32[12,128,128]{2,1,0:T(8,128)S(1)} fusion(f32[12,128,256]{2,1,0:T(8,128)} %gather_fusion, f32[12,128,256]{2,1,0:T(8,128)S(1)} %gather_fusion.1, s32[24,128,128]{2,1,0:T(8,128)} %param.11, s32[]{:T(128)S(6)} %select_n.58), kind=kOutput, calls=%fused_computation.26 | convolution fusion | flops 604372992 | bytes 4718596 | tf_op jit(solution)/shard_map/while/body/eval_jaxpr/bik,bjk->bij/dot_general | solution.py:73
  28.4 2.7 %fusion.51 = f32[12,128,256]{2,1,0:T(8,128)} fusion(f32[12,128,128]{2,1,0:T(8,128)S(1)} %convolution_multiply_fusion.3, f32[12,128,256]{2,1,0:T(8,128)S(1)} %gather_fusion.1), kind=kOutput, calls=%fused_computation.81 | convolution fusion | flops 603979776 | bytes 3932160 | tf_op jit(solution)/shard_map/while/body/eval_jaxpr/bij,bjk->bik/dot_general | solution.py:76
  31.1 1.9 fusion.53
  33.2 1.8 gather_fusion.2
  35.1 3.5 %fusion.17 = f32[8,128,256]{2,1,0:T(8,128)} fusion(f32[8,128,256]{2,1,0:T(8,128)S(1)} %copy-done.20, f32[8,128,128]{2,1,0:T(8,128)S(1)} %bitcast.118, f32[1,128,256]{2,1,0:T(8,128)S(1)} %bitcast.133, f32[7,128,256]{2,1,0:T(8,128)} %bitcast.129, f32[7,128,256]{2,1,0:T(8,128)} %fusion.53, f32[1,128,256]{2,1,0:T(8,128)} %bitcast.16), kind=kOutput, calls=%fused_computation.21 | convolution fusion | flops 403701760 | bytes 4718592 | tf_op jit(solution)/shard_map/bij,bjk->bik/dot_general | solution.py:56
  38.6 0.6 gather_fusion.3
  39.3 3.8 %convolution_multiply_fusion.2 = f32[12,128,128]{2,1,0:T(8,128)S(1)} fusion(f32[12,128,256]{2,1,0:T(8,128)} %gather_fusion.2, f32[12,128,256]{2,1,0:T(8,128)S(1)} %gather_fusion.3, s32[24,128,128]{2,1,0:T(8,128)} %param.11, s32[]{:T(128)S(6)} %select_n.62), kind=kOutput, calls=%fused_computation.25 | convolution fusion | flops 604372992 | bytes 4718596 | tf_op jit(solution)/shard_map/bik,bjk->bij/dot_general | solution.py:73
  43.1 1.5 fusion.52
  44.7 1.9 fusion.4
  46.5 1.7 fusion.8
  48.6 0.9 copy-done.7
  49.5 1.1 multiply_reduce_fusion.2
  50.5 40.9 %all-reduce = (f32[]{:T(128)}, f32[]{:T(128)}) all-reduce(f32[]{:T(128)} %get-tuple-element.43, f32[]{:T(128)} %get-tuple-element.42), channel_id=1, replica_groups=mesh['row'=16,'loop'=2] {'row','loop'}, use_global_device_ids=true, to_apply=%region_1.0 | all-reduce | flops 2 | bytes 16 | tf_op jit(solution)/shard_map/psum | solution.py:25
  92.7 3.1 %multiply_reduce_fusion.1 = (f32[]{:T(128)}, f32[1024,256]{1,0:T(8,128)}) fusion(f32[1024,256]{1,0:T(8,128)S(1)} %copy-done, f32[8,128,256]{2,1,0:T(8,128)} %fusion.17, f32[1024]{0:T(1024)S(1)} %fusion.31, f32[8,128,256]{2,1,0:T(8,128)S(1)} %copy.11, f32[]{:T(128)S(6)} %div.9), kind=kLoop, calls=%fused_computation.42 | loop fusion | flops 1835007 | bytes 4198408 | tf_op jit(solution)/shard_map/reduce_sum | solution.py:25
  95.8 40.5 %psum.30 = f32[]{:T(128)} all-reduce(f32[]{:T(128)} %get-tuple-element.46), channel_id=1, replica_groups=mesh['row'=16,'loop'=2] {'row','loop'}, use_global_device_ids=true, to_apply=%region_9.10 | all-reduce | flops 1 | bytes 8 | tf_op jit(solution)/shard_map/psum | solution.py:25
  137.5 1.4 multiply_add_fusion.1
  138.9 1.8 gather_fusion.5
  140.7 1.8 gather_fusion.4
  142.7 0.9 copy-done.12
  143.7 1.1 fusion.44
  145.7 1.6 convolution_multiply_fusion
  147.4 1.5 fusion.55
  148.9 1.7 fusion
  150.7 1.6 convolution_multiply_fusion.1
  152.4 1.5 fusion.54
  153.9 1.4 collective-permute-start.4
  155.3 5.0 %collective-permute-start.5 = (f32[128,256]{1,0:T(8,128)S(1)}, f32[128,256]{1,0:T(8,128)S(1)}, u32[]{:S(2)}, u32[]{:S(2)}) collective-permute-start(f32[128,256]{1,0:T(8,128)S(1)} %convolution_bitcast_fusion.3), channel_id=1, source_target_pairs={{0,1},{1,2},{2,3},{3,4},{4,5},{5,6},{6,7},{7,8},{8,9},{9,10},{10,1... | collective-permute-start | bytes 393224 | tf_op jit(solution)/shard_map/ppermute | solution.py:21
  160.3 1.7 fusion.11
  162.1 1.0 convolution_bitcast_fusion.2
  163.4 0.6 collective-permute-done.5
  164.0 1.1 fusion.15
  165.2 1.0 copy-done.8
  166.2 1.0 multiply_reduce_fusion
  167.2 40.6 %psum.31 = f32[]{:T(128)} all-reduce(f32[]{:T(128)} %multiply_reduce_fusion), channel_id=1, replica_groups=mesh['row'=16,'loop'=2] {'row','loop'}, use_global_device_ids=true, to_apply=%region_11.12 | all-reduce | flops 1 | bytes 8 | tf_op jit(solution)/shard_map/psum | solution.py:25
  209.2 3.5 %multiply_subtract_fusion = (f32[1024,256]{1,0:T(8,128)}, f32[1024,256]{1,0:T(8,128)}) fusion(f32[1024,256]{1,0:T(8,128)} %get-tuple-element.47, f32[]{:T(128)S(6)} %div.11, f32[8,128,256]{2,1,0:T(8,128)} %copy-done.8, f32[1024,256]{1,0:T(8,128)S(1)} %multiply_add_fusion.1, f32[1024]{0:T(1024)S(1)} %fusion.31, f32[8,128,256]{2,1,0:T(8,128)} %copy-done.6, ...), kind=kLoop, calls=%fused_computation.38 | loop fusion | flops 2097152 | bytes 7344136 | tf_op jit(solution)/shard_map/sub | solution.py:94
  (68 shorter events, 2.8 us)
Async XLA Ops:
  0.6 17.0 %copy-start = (f32[1024,256]{1,0:T(8,128)S(1)}, f32[1024,256]{1,0:T(8,128)}, u32[]{:S(2)}) copy-start(f32[1024,256]{1,0:T(8,128)} %param.8) | copy-start | bytes 3145732
  0.6 38.0 %collective-permute-start = (f32[256,256]{1,0:T(8,128)}, f32[256,256]{1,0:T(8,128)S(1)}, u32[]{:S(2)}, u32[]{:S(2)}) collective-permute-start(f32[256,256]{1,0:T(8,128)} %param.7), channel_id=1, source_target_pairs={{0,1},{1,0},{2,3},{3,2},{4,5},{5,4},{6,7},{7,6},{8,9},{9,8},{10,11... | collective-permute-start | bytes 786440 | tf_op jit(solution)/shard_map/while/body/eval_jaxpr/ppermute | solution.py:15
  5.2 29.9 %collective-permute-start.2 = (f32[128,256]{1,0:T(8,128)}, f32[128,256]{1,0:T(8,128)S(1)}, u32[]{:S(2)}, u32[]{:S(2)}) collective-permute-start(f32[128,256]{1,0:T(8,128)} %slice.59), channel_id=1, source_target_pairs={{1,0},{2,1},{3,2},{4,3},{5,4},{6,5},{7,6},{8,7},{9,8},{10,9},{11,1... | collective-permute-start | bytes 393224 | tf_op jit(solution)/shard_map/ppermute | solution.py:21
  8.4 26.7 %collective-permute-start.3 = (f32[128,256]{1,0:T(8,128)}, f32[128,256]{1,0:T(8,128)}, u32[]{:S(2)}, u32[]{:S(2)}) collective-permute-start(f32[128,256]{1,0:T(8,128)} %fusion.26), channel_id=1, source_target_pairs={{0,1},{1,2},{2,3},{3,4},{4,5},{5,6},{6,7},{7,8},{8,9},{9,10},{10,1... | collective-permute-start | bytes 393224 | tf_op jit(solution)/shard_map/ppermute | solution.py:21
  14.5 20.6 %collective-permute-start.1 = (f32[128]{0:T(128)S(1)}, f32[128]{0:T(128)S(1)}, u32[]{:S(2)}, u32[]{:S(2)}) collective-permute-start(f32[128]{0:T(128)S(1)} %slice_reduce_fusion), channel_id=1, source_target_pairs={{0,1},{1,2},{2,3},{3,4},{4,5},{5,6},{6,7},{7,8},{8,9},{9,10},{10,1... | collective-permute-start | bytes 1544 | tf_op jit(solution)/shard_map/ppermute | solution.py:21
  17.6 1.4 copy-start.24
  17.6 1.4 copy-start.25
  17.6 2.0 copy-start.11
  19.8 2.3 %copy-start.13 = (f32[8,128,128]{1,2,0:T(8,128)}, f32[8,128,128]{1,2,0:T(8,128)S(1)}, u32[]{:S(2)}) copy-start(f32[8,128,128]{1,2,0:T(8,128)S(1)} %copy.12) | copy-start | bytes 1572868
  22.1 1.8 copy-start.9
  24.6 3.8 %copy-start.1 = (f32[12,128,256]{2,1,0:T(8,128)}, f32[12,128,256]{2,1,0:T(8,128)S(1)}, u32[]{:S(2)}) copy-start(f32[12,128,256]{2,1,0:T(8,128)S(1)} %gather_fusion.1) | copy-start | bytes 4718596
  28.4 2.7 %copy-start.15 = (f32[896,128]{1,0:T(8,128)S(1)}, f32[896,128]{1,0:T(8,128)}, u32[]{:S(2)}) copy-start(f32[896,128]{1,0:T(8,128)} %slice.55) | copy-start | bytes 1376260
  28.4 2.7 %copy-start.21 = (f32[896,256]{1,0:T(8,128)S(1)}, f32[896,256]{1,0:T(8,128)}, u32[]{:S(2)}) copy-start(f32[896,256]{1,0:T(8,128)} %get-tuple-element.66) | copy-start | bytes 2752516
  31.1 1.9 copy-start.5
  33.2 1.9 copy-start.20
  39.3 3.8 %copy-start.3 = (f32[12,128,256]{2,1,0:T(8,128)}, f32[12,128,256]{2,1,0:T(8,128)S(1)}, u32[]{:S(2)}) copy-start(f32[12,128,256]{2,1,0:T(8,128)S(1)} %gather_fusion.3) | copy-start | bytes 4718596
  43.1 1.5 copy-start.23
  44.6 1.9 copy-start.10
  44.7 1.9 copy-start.22
  48.2 1.2 copy-start.7
  142.5 1.0 copy-start.12
  142.5 1.2 copy-start.14
  142.5 2.6 %copy-start.19 = (f32[12,128,256]{2,1,0:T(8,128)S(1)}, f32[12,128,256]{2,1,0:T(8,128)}, u32[]{:S(2)}) copy-start(f32[12,128,256]{2,1,0:T(8,128)} %gather_fusion.5) | copy-start | bytes 4718596
  143.7 1.5 copy-start.4
  143.7 2.0 copy-start.17
  148.8 1.7 copy-start.2
  148.9 1.9 copy-start.18
  153.8 8.2 %copy-start.16 = (f32[896,128]{1,0:T(8,128)S(1)}, f32[896,128]{1,0:T(8,128)}, u32[]{:S(2)}) copy-start(f32[896,128]{1,0:T(8,128)} %slice.55) | copy-start | bytes 1376260
  153.9 9.6 %collective-permute-start.4 = (f32[128,256]{1,0:T(8,128)S(1)}, f32[128,256]{1,0:T(8,128)S(1)}, u32[]{:S(2)}, u32[]{:S(2)}) collective-permute-start(f32[128,256]{1,0:T(8,128)S(1)} %slice.82), channel_id=1, source_target_pairs={{1,0},{2,1},{3,2},{4,3},{5,4},{6,5},{7,6},{8,7},{9,8},{10,9},{11,1... | collective-permute-start | bytes 393224 | tf_op jit(solution)/shard_map/ppermute | solution.py:21
  155.3 8.8 %collective-permute-start.5 = (f32[128,256]{1,0:T(8,128)S(1)}, f32[128,256]{1,0:T(8,128)S(1)}, u32[]{:S(2)}, u32[]{:S(2)}) collective-permute-start(f32[128,256]{1,0:T(8,128)S(1)} %convolution_bitcast_fusion.3), channel_id=1, source_target_pairs={{0,1},{1,2},{2,3},{3,4},{4,5},{5,6},{6,7},{7,8},{8,9},{9,10},{10,1... | collective-permute-start | bytes 393224 | tf_op jit(solution)/shard_map/ppermute | solution.py:21
  163.4 1.8 copy-start.6
  165.2 1.0 copy-start.8
where the time goes:
time: 214 us; the launch traced here: 213 us
  blocking collectives  122 us (57%)
  matrix products  37.7 us (18%)
  local copies, waits for them, and re-layouts  18.1 us (8%)
  starting transfers between devices  17.2 us (8%)
  other arithmetic  12 us (6%)
  between operations  5.05 us (2%)
    psum x3, blocking collectives, global_sum(): return lax.psum(jnp.sum(values), ('row', 'loop'))  122 us
    ppermute x5, starting transfers between devices, from_behind_2(): lax.ppermute(value, axis, [(source, source + steps) for source in range(i...  14.2 us
    dot_general x4, matrix products, panel_term(): jnp.einsum('bik,bjk->bij', left_tiles, right_tiles, precision=highest)  10.9 us
    gather x4, local copies, waits for them, and re-layouts, panel_term(): left_tiles = user_tiles[chosen_users]  7.34 us
    dot_general x4, matrix products, panel_term(): contrib = jnp.einsum('bij,bjk->bik', scores, right_tiles, precision=highest)  7.07 us
    dot_general x4, matrix products, panel_term(): return jnp.einsum('bn,bik->nik', selector, contrib, precision=highest)  6.91 us
    reduce_sum x3, other arithmetic, global_sum(): return lax.psum(jnp.sum(values), ('row', 'loop'))  5.2 us
    dot_general x2, matrix products, body(): jnp.einsum('bij,bjk->bik', onward, following, precision=highest)  4.65 us
  transfers between devices with their start and end apart: 6, of which 1 were waited for; matrix products, arithmetic and copies ran while one was open for 14% of the time, Pallas kernels for 0%

commit v1 on v0

v1 whole, which is shorter than its diff:
```python
import functools

import jax
import jax.numpy as jnp
from jax import lax
from jax.experimental import pallas as pl
from jax.experimental.pallas import tpu as pltpu
from jax.sharding import PartitionSpec as P

ridge_weight = 0.5
MESH = pl.DeviceIdType.MESH
F32 = jnp.float32
BF16 = jnp.bfloat16
COUNT_BITS = 4
NN = (((1,), (0,)), ((), ()))
NT = (((1,), (1,)), ((), ()))
TN = (((0,), (0,)), ((), ()))


def halves(x):
    high = x.astype(BF16)
    return high, (x - high.astype(F32)).astype(BF16)


def dot3(a, b, dims):
    dot = functools.partial(lax.dot_general, dimension_numbers=dims, preferred_element_type=F32)
    return dot(a[0], b[0]) + (dot(a[1], b[0]) + dot(a[0], b[1]))


def lanes(x):
    rows, width = x.shape
    x = sum(x[:, c : c + 128] for c in range(0, width, 128))
    return jnp.sum(x, axis=0, keepdims=True)


def kernel(
    sizes,
    users_ref,
    items_ref,
    panel_ref,
    right_ref,
    mask_ref,
    self_ref,
    next_ref,
    q_out,
    p_out,
    coef_out,
    b_v,
    q_v,
    p_v,
    v_hi,
    v_lo,
    panel_v,
    h_hi,
    h_lo,
    mask_v,
    packed,
    self_v,
    next_v,
    w_hi,
    w_lo,
    diag,
    ahead,
    carried,
    product,
    columns_out,
    columns_in,
    mine,
    near,
    near_sum,
    far,
    local_sem,
    panel_s,
    panel_r,
    share_s,
    share_r,
    halo_s,
    halo_r,
    near_s,
    near_r,
    far_s,
    far_r,
):
    R, L, g, T, U, K, PR, per_panel = sizes
    Z = R // g
    G = g * L
    row, loop = lax.axis_index("row"), lax.axis_index("loop")
    n = R * L
    d = row * L + loop
    me_near = lax.rem(row, g) * L + loop
    me_far = row // g
    quarter = lax.rem(row, g)
    base = me_far * g
    after, before = lax.rem(d + 1, n), lax.rem(d + n - 1, n)
    after = (after // L, lax.rem(after, L))
    before = (before // L, lax.rem(before, L))
    has_after, has_before = d < n - 1, d > 0
    tail = (U - 1) * T

    loads = [
        pltpu.make_async_copy(src, dst, local_sem.at[i])
        for i, (src, dst) in enumerate(
            [
                (next_ref, next_v),
                (right_ref, b_v),
                (self_ref, self_v),
                (panel_ref, panel_v.at[0]),
                (mask_ref, mask_v),
            ]
        )
    ]
    for load in loads:
        load.start()

    def near_device(i):
        t = lax.rem(me_near + i, G)
        return t, (base + t // L, lax.rem(t, L))

    def far_device(i):
        t = lax.rem(me_far + i, Z)
        return t, (t * g + quarter, loop)

    barrier = pltpu.get_barrier_semaphore()
    greeted = [near_device(i)[1] for i in range(1, G)] + [far_device(i)[1] for i in range(1, Z)]
    greeted += [after, before]
    for device in greeted:
        pl.semaphore_signal(barrier, inc=1, device_id=device, device_id_type=MESH)
    pl.semaphore_wait(barrier, len(greeted))

    def remote(src, dst, send, recv, device):
        return pltpu.make_async_remote_copy(
            src_ref=src, dst_ref=dst, send_sem=send, recv_sem=recv, device_id=device, device_id_type=MESH
        )

    part = PR // g

    def share(k, which):
        return panel_v.at[k, pl.ds(pl.multiple_of(which * part, part), part)]

    own_share = panel_ref.at[pl.ds(pl.multiple_of(quarter * part, part), part)]
    direct = [
        remote(own_share, share(k, quarter), panel_s.at[k], panel_r.at[k], (row, lax.rem(loop + L - k, L)))
        for k in range(1, L)
    ]
    for copy in direct:
        copy.start()

    def forwards(k):
        copies = []
        for i in range(1, g):
            t = lax.rem(quarter + i, g)
            copies.append(
                remote(share(k, quarter), share(k, quarter), share_s.at[k, i], share_r.at[k, quarter], (base + t, loop))
            )
        return copies

    def forward_in(k, i):
        t = lax.rem(quarter + i, g)
        return remote(share(k, t), share(k, t), share_s.at[k, i], share_r.at[k, t], (base + t, loop))

    first_0 = remote(right_ref.at[pl.ds(0, T)], ahead.at[0], halo_s.at[0, 0], halo_r.at[0, 0], before)
    first_1 = remote(q_v.at[pl.ds(0, T)], ahead.at[1], halo_s.at[1, 0], halo_r.at[1, 0], before)
    product_copies = [
        remote(product.at[ph], carried.at[ph], halo_s.at[ph, 1], halo_r.at[ph, 1], after) for ph in range(2)
    ]
    columns_copy = remote(columns_out, columns_in, halo_s.at[0, 2], halo_r.at[0, 2], after)

    @pl.when(has_before)
    def _():
        first_0.start()

    @pl.when(jnp.logical_not(has_before))
    def _():
        carried[...] = jnp.zeros_like(carried)
        columns_in[...] = jnp.zeros_like(columns_in)

    @pl.when(jnp.logical_not(has_after))
    def _():
        ahead[...] = jnp.zeros_like(ahead)

    loads[0].wait()
    loads[1].wait()
    last_next = next_v[tail:]
    columns_out[...] = jnp.broadcast_to(jnp.sum(last_next, axis=0, keepdims=True), columns_out.shape)
    last_turned = halves(last_next.T)
    product[0] = dot3(last_turned, halves(b_v[tail:]), NN)

    @pl.when(has_after)
    def _():
        columns_copy.start()
        product_copies[0].start()

    loads[2].wait()
    degrees = []
    onward_columns = None
    for b in range(U):
        rows = slice(b * T, (b + 1) * T)
        own = self_v[rows]
        sym = 0.5 * (own + own.T)
        onward = next_v[rows]
        turned = onward.T
        degree = jnp.sum(sym, axis=1, keepdims=True) + jnp.sum(onward, axis=1, keepdims=True)
        if onward_columns is not None:
            degree = degree + onward_columns
        onward_columns = jnp.sum(turned, axis=1, keepdims=True)
        diag[rows] = jnp.broadcast_to(degree + ridge_weight, (T, T))
        for place, tile, target in ((1, sym, b), (2, onward, b), (0, turned, b + 1)):
            if target < U:
                high, low = halves(tile)
                w_hi[target, :, place * T : (place + 1) * T] = high
                w_lo[target, :, place * T : (place + 1) * T] = low

    def split_field(ref):
        for b in range(U):
            rows = slice(b * T, (b + 1) * T)
            v_hi[rows], v_lo[rows] = halves(ref[rows])

    def split_panel(k):
        h_hi[k], h_lo[k] = halves(panel_v[k])

    def inner(b, field):
        low_block, high_block = max(b - 1, 0), min(b + 2, U)
        span = slice(low_block * T, high_block * T)
        cols = slice((low_block - b + 1) * T, (high_block - b + 1) * T)
        coupled = dot3((w_hi[b, :, cols], w_lo[b, :, cols]), (v_hi[span], v_lo[span]), NN)
        rows = slice(b * T, (b + 1) * T)
        scale = diag[rows]
        return jnp.concatenate([scale] * (K // T), axis=1) * field[rows] - coupled

    def pack(k):
        panel_index = lax.rem(loop + k, L)
        sums = [jnp.zeros((T, T), jnp.int32)] * (PR // T)
        for e in range(per_panel):
            at = panel_index * per_panel + e
            seen = mask_v[at] != 0
            unit = jnp.left_shift(jnp.int32(1), users_ref[at] * COUNT_BITS)
            for c in range(PR // T):
                weight = jnp.where(items_ref[at] == c, unit, 0)
                sums[c] = sums[c] + jnp.where(seen, weight, 0)
        for c in range(PR // T):
            packed[k, :, c * T : (c + 1) * T] = sums[c]

    def gram(k, blocks):
        rows = slice(blocks[0] * T, (blocks[-1] + 1) * T)
        panel = (h_hi[k], h_lo[k])
        scores = dot3((v_hi[rows], v_lo[rows]), panel, NT)
        counts = []
        for b in blocks:
            word = packed[k]
            if b:
                word = lax.shift_right_logical(word, jnp.int32(COUNT_BITS * b))
            counts.append((word & ((1 << COUNT_BITS) - 1)).astype(F32))
        scores = scores * jnp.concatenate(counts, axis=0)
        return dot3(halves(scores), panel, NN)

    split_field(b_v)
    pairs = [(0, 1)] + [(U - 2, U - 1)] + [(b, b + 1) for b in range(2, U - 2, 2)]

    for b in range(U):
        q_v[b * T : (b + 1) * T] = inner(b, b_v)

    passed = []
    for k in range(1, L):
        direct[k - 1].wait_recv()
        passed += forwards(k)
        for copy in passed[-(g - 1) :] if g > 1 else []:
            copy.start()

    loads[3].wait()
    split_panel(0)
    loads[4].wait()
    for k in range(L):
        pack(k)

    def add_gram(k, blocks, out):
        rows = slice(blocks[0] * T, (blocks[-1] + 1) * T)
        out[rows] = out[rows] + gram(k, blocks)

    for blocks in pairs:
        add_gram(0, blocks, q_v)
    for k in range(1, L):
        for i in range(1, g):
            forward_in(k, i).wait_recv()
        split_panel(k)
    for blocks in pairs[:2]:
        for k in range(1, L):
            add_gram(k, blocks, q_v)

    def edges(ph, out):
        @pl.when(has_before)
        def _():
            product_copies[ph].wait_recv()

        out[:T] = out[:T] - carried[ph]

        @pl.when(has_after)
        def _():
            (first_0, first_1)[ph].wait_recv()

        tile = (w_hi[U - 1, :, 2 * T :], w_lo[U - 1, :, 2 * T :])
        out[tail:] = out[tail:] - dot3(tile, halves(ahead[ph]), NN)

    @pl.when(has_before)
    def _():
        columns_copy.wait_recv()

    entering = jnp.broadcast_to(columns_in[:1], (T, T)).T
    diag[:T] = diag[:T] + entering
    q_v[:T] = q_v[:T] + jnp.concatenate([entering] * (K // T), axis=1) * b_v[:T]
    edges(0, q_v)

    @pl.when(has_before)
    def _():
        first_1.start()

    product[1] = dot3(last_turned, halves(q_v[tail:]), NN)

    @pl.when(has_after)
    def _():
        product_copies[1].start()

    for blocks in pairs[2:]:
        for k in range(1, L):
            add_gram(k, blocks, q_v)

    def store_sums(ph, rows_of_lanes):
        pad = [jnp.zeros((8 - len(rows_of_lanes), 128), F32)]
        mine[ph] = jnp.concatenate(rows_of_lanes + pad, axis=0)

    def near_copy(ph, i, sending):
        t, device = near_device(i)
        slot = me_near if sending else t
        return remote(mine.at[ph], near.at[ph, slot], near_s.at[ph, i], near_r.at[ph, slot], device)

    def far_copy(ph, i, sending):
        t, device = far_device(i)
        slot = me_far if sending else t
        return remote(near_sum.at[ph], far.at[ph, slot], far_s.at[ph, i], far_r.at[ph, slot], device)

    def start_near(ph):
        for i in range(1, G):
            near_copy(ph, i, True).start()

    def near_to_far(ph):
        total = mine[ph]
        for i in range(1, G):
            copy = near_copy(ph, i, False)
            copy.wait_recv()
            total = total + near[ph, lax.rem(me_near + i, G)]
        near_sum[ph] = total
        for i in range(1, Z):
            far_copy(ph, i, True).start()

    def finish_far(ph):
        total = near_sum[ph]
        for i in range(1, Z):
            far_copy(ph, i, False).wait_recv()
            total = total + far[ph, lax.rem(me_far + i, Z)]
        return jnp.sum(total, axis=1, keepdims=True)

    norm = jnp.zeros((1, 128), F32)
    energy = jnp.zeros((1, 128), F32)
    for b in range(U):
        rows = slice(b * T, (b + 1) * T)
        norm = norm + lanes(b_v[rows] * b_v[rows])
        energy = energy + lanes(b_v[rows] * q_v[rows])
    store_sums(0, [norm, energy])
    start_near(0)
    q_copy = pltpu.make_async_copy(q_v, q_out, local_sem.at[5])
    q_copy.start()

    split_field(q_v)
    for b in range(U):
        p_v[b * T : (b + 1) * T] = inner(b, q_v)
    for blocks in pairs:
        add_gram(0, blocks, p_v)
    near_to_far(0)
    for blocks in pairs:
        for k in range(1, L):
            add_gram(k, blocks, p_v)
    edges(1, p_v)
    p_copy = pltpu.make_async_copy(p_v, p_out, local_sem.at[6])
    p_copy.start()

    sums = finish_far(0)
    norm_0, energy_0 = sums[0:1], sums[1:2]
    step_0 = norm_0 / energy_0
    norm = jnp.zeros((1, 128), F32)
    energy = jnp.zeros((1, 128), F32)
    cross = jnp.zeros((1, 128), F32)
    for b in range(U):
        rows = slice(b * T, (b + 1) * T)
        image = q_v[rows]
        residual = b_v[rows] - step_0 * image
        norm = norm + lanes(residual * residual)
        energy = energy + lanes(residual * (image - step_0 * p_v[rows]))
        cross = cross + lanes(residual * image)
    store_sums(1, [norm, energy, cross])
    start_near(1)
    near_to_far(1)
    sums = finish_far(1)
    norm_1, energy_1, cross_1 = sums[0:1], sums[1:2], sums[2:3]
    beta = norm_1 / norm_0
    step_1 = norm_1 / (energy_1 + 2.0 * beta * cross_1 + beta * beta * energy_0)
    first = step_0 + step_1 * (1.0 + beta)
    second = step_0 * step_1
    coef_out[...] = jnp.concatenate([jnp.broadcast_to(first, (4, 128)), jnp.broadcast_to(second, (4, 128))], axis=0)

    for copy in direct + passed:
        copy.wait_send()
    for ph in range(2):
        for i in range(1, G):
            near_copy(ph, i, True).wait_send()
        for i in range(1, Z):
            far_copy(ph, i, True).wait_send()

    @pl.when(has_before)
    def _():
        first_0.wait_send()
        first_1.wait_send()

    @pl.when(has_after)
    def _():
        columns_copy.wait_send()
        for copy in product_copies:
            copy.wait_send()

    q_copy.wait()
    p_copy.wait()


def body(panels, right_side, block_users, block_items, masks, self_tiles, next_tiles):
    R, L = lax.axis_size("row"), lax.axis_size("loop")
    g = 4 if R % 4 == 0 else R
    Z, G = R // g, 4 * L if R % 4 == 0 else R * L
    T = masks.shape[1]
    PR, K = panels.shape
    rows = right_side.shape[0]
    U = rows // T
    entries = masks.shape[0]
    per_panel = entries // L
    assert per_panel < 1 << COUNT_BITS and U * COUNT_BITS <= 32
    sizes = (R, L, g, T, U, K, PR, per_panel)
    hbm = pl.BlockSpec(memory_space=pl.ANY)
    smem = pl.BlockSpec(memory_space=pltpu.SMEM)
    vmem = pl.BlockSpec(memory_space=pltpu.VMEM)
    field = jax.ShapeDtypeStruct((rows, K), F32)
    dma = pltpu.SemaphoreType.DMA
    q, p, coef = pl.pallas_call(
        functools.partial(kernel, sizes),
        out_shape=(field, field, jax.ShapeDtypeStruct((8, 128), F32)),
        in_specs=[smem, smem] + [hbm] * 5,
        out_specs=(hbm, hbm, vmem),
        scratch_shapes=[
            pltpu.VMEM((rows, K), F32),
            pltpu.VMEM((rows, K), F32),
            pltpu.VMEM((rows, K), F32),
            pltpu.VMEM((rows, K), BF16),
            pltpu.VMEM((rows, K), BF16),
            pltpu.VMEM((L, PR, K), F32),
            pltpu.VMEM((L, PR, K), BF16),
            pltpu.VMEM((L, PR, K), BF16),
            pltpu.VMEM((entries, T, T), jnp.int32),
            pltpu.VMEM((L, T, PR), jnp.int32),
            pltpu.VMEM((rows, T), F32),
            pltpu.VMEM((rows, T), F32),
            pltpu.VMEM((U, T, 3 * T), BF16),
            pltpu.VMEM((U, T, 3 * T), BF16),
            pltpu.VMEM((rows, T), F32),
            pltpu.VMEM((2, T, K), F32),
            pltpu.VMEM((2, T, K), F32),
            pltpu.VMEM((2, T, K), F32),
            pltpu.VMEM((8, T), F32),
            pltpu.VMEM((8, T), F32),
            pltpu.VMEM((2, 8, 128), F32),
            pltpu.VMEM((2, G, 8, 128), F32),
            pltpu.VMEM((2, 8, 128), F32),
            pltpu.VMEM((2, Z, 8, 128), F32),
            dma((7,)),
            dma((L,)),
            dma((L,)),
            dma((L, g)),
            dma((L, g)),
            dma((2, 3)),
            dma((2, 3)),
            dma((2, G)),
            dma((2, G)),
            dma((2, Z)),
            dma((2, Z)),
        ],
        compiler_params=pltpu.CompilerParams(
            collective_id=0, has_side_effects=True, vmem_limit_bytes=32 * 1024 * 1024
        ),
        cost_estimate=pl.CostEstimate(flops=8 * rows * K * PR * L, bytes_accessed=8 * rows * K * 4, transcendentals=0),
    )(block_users, block_items, panels, right_side, masks, self_tiles, next_tiles)
    first, second = coef[0, 0], coef[4, 0]
    solution_field = first * right_side - second * q
    residual = right_side - first * q + second * p
    return solution_field, residual


def solution(mesh):
    placed = (
        P("loop", None),
        P(("row", "loop"), None),
        P(("row", "loop")),
        P(("row", "loop")),
        P(("row", "loop"), None, None),
        P(("row", "loop"), None),
        P(("row", "loop"), None),
    )
    return jax.shard_map(
        body,
        mesh=mesh,
        in_specs=placed,
        out_specs=(P(("row", "loop"), None), P(("row", "loop"), None)),
        check_vma=False,
    )
```

time: 214 us -> 47.6 us (0.22)
  blocking collectives: 122 us -> 0 us
  matrix products: 37.7 us -> 0 us
  Pallas kernels: 0 us -> 36.2 us
  starting transfers between devices: 17.2 us -> 0 us
  local copies, waits for them, and re-layouts: 18.1 us -> 7.53 us
  other arithmetic: 12 us -> 2.82 us
  between operations: 5.05 us -> 0.66 us
    psum x3 -> x0, blocking collectives: 122 us -> none  [global_sum(): return lax.psum(jnp.sum(values), ('row', 'loop'))]
    dot_general x20 -> x0, matrix products: 37.7 us -> none  [the longest x4 10.9 us: panel_term(): jnp.einsum('bik,bjk->bij', left_tiles, right_tiles, precision=highest)]
    pallas_call x0 -> x1, Pallas kernels: none -> 36.2 us  [body(): pl.pallas_call(functools.partial(kernel, sizes), out_shape=(field, field,...]
    ppermute x6 -> x0, starting transfers between devices: 17.2 us -> none  [the longest x5 14.2 us: from_behind_2(): lax.ppermute(value, axis, [(source, source + steps) for source in range(i...]
    gather x6 -> x0, local copies, waits for them, and re-layouts: 8.64 us -> none  [the longest x4 7.34 us: panel_term(): left_tiles = user_tiles[chosen_users]]
    reduce_sum x7 -> x0, other arithmetic: 6.52 us -> none  [the longest x3 5.2 us: global_sum(): return lax.psum(jnp.sum(values), ('row', 'loop'))]
    slice x5 -> x1, local copies, waits for them, and re-layouts: 4.92 us -> 0.57 us  [body(): first, second = (coef[0, 0], coef[4, 0])]
    sub x1 -> x0, other arithmetic: 3.51 us -> none  [body(): residual = residual - step_size * image]
  transfers between devices with their start and end apart: 6 -> 0, of which waited for: 1 -> 0; matrix products, arithmetic and copies ran while one was open for 14% -> 0% of each run, Pallas kernels for 0% -> 0%
where the time goes in v1:
time: 47.6 us; the launch traced here: 47.2 us
  Pallas kernels  36.2 us (76%)
  local copies, waits for them, and re-layouts  7.53 us (16%)
  other arithmetic  2.82 us (6%)
  between operations  0.66 us (1%)
    pallas_call x1, Pallas kernels, body(): pl.pallas_call(functools.partial(kernel, sizes), out_shape=(field, field,...  36.2 us
    unnamed x14, local copies, waits for them, and re-layouts  6.97 us
    add x1, other arithmetic, body(): residual = right_side - first * q + second * p  2.82 us

profile of v1, /device:TPU:0, one launch (start us, length us, event | category | flops | bytes accessed | tf_op | source)
XLA Modules:
  0.0 47.2 jit_solution(18350456989404116197)
XLA Ops:
  0.6 0.0 copy-start
  0.6 1.2 %copy-done = f32[1024,256]{1,0:T(8,128)S(1)} copy-done((f32[1024,256]{1,0:T(8,128)S(1)}, f32[1024,256]{1,0:T(8,128)}, u32[]{:S(2)}) %copy-start) | copy-done | bytes 1048600
  1.9 0.0 copy-start.1
  1.9 1.4 %copy-done.1 = s32[24,128,128]{2,1,0:T(8,128)S(1)} copy-done((s32[24,128,128]{2,1,0:T(8,128)S(1)}, s32[24,128,128]{2,1,0:T(8,128)}, u32[]{:S(2)}) %copy-start.1) | copy-done | bytes 1572888
  3.3 0.0 copy-start.2
  3.3 1.0 %copy-done.2 = f32[1024,128]{1,0:T(8,128)S(1)} copy-done((f32[1024,128]{1,0:T(8,128)S(1)}, f32[1024,128]{1,0:T(8,128)}, u32[]{:S(2)}) %copy-start.2) | copy-done | bytes 524312
  4.3 0.0 copy-start.3
  4.3 1.0 %copy-done.3 = f32[1024,128]{1,0:T(8,128)S(1)} copy-done((f32[1024,128]{1,0:T(8,128)S(1)}, f32[1024,128]{1,0:T(8,128)}, u32[]{:S(2)}) %copy-start.3) | copy-done | bytes 524312
  5.4 0.0 copy-start.4
  5.4 0.9 %copy-done.4 = f32[256,256]{1,0:T(8,128)S(1)} copy-done((f32[256,256]{1,0:T(8,128)S(1)}, f32[256,256]{1,0:T(8,128)}, u32[]{:S(2)}) %copy-start.4) | copy-done | bytes 262168
  6.3 0.0 copy-start.5
  6.3 0.7 %copy-done.5 = s32[24]{0:T(128)S(1)} copy-done((s32[24]{0:T(128)S(1)}, s32[24]{0:T(128)}, u32[]{:S(2)}) %copy-start.5) | copy-done | bytes 120
  7.0 0.0 copy-start.6
  7.0 0.7 %copy-done.6 = s32[24]{0:T(128)S(1)} copy-done((s32[24]{0:T(128)S(1)}, s32[24]{0:T(128)}, u32[]{:S(2)}) %copy-start.6) | copy-done | bytes 120
  7.6 36.2 %shard_map.86 = (f32[1024,256]{1,0:T(8,128)S(1)}, f32[1024,256]{1,0:T(8,128)S(1)}, f32[8,128]{1,0:T(8,128)S(1)}) custom-call(s32[24]{0:T(128)S(1)} %copy-done.5, s32[24]{0:T(128)S(1)} %copy-done.6, f32[256,256]{1,0:T(8,128)S(1)} %copy-done.4, f32[1024,256]{1,0:T(8,128)S(1)} %copy-done, s32[24,128,128]{2,1,0:T(8,128)S(1)} %copy-done.1, ...), custom_call_target="tpu_custom_call" | custom-call | flops 1073741824 | bytes 8388608 | tf_op jit(solution)/shard_map/pallas_call | solution.py:449
  43.8 0.6 %fusion = (f32[1,1]{1,0:T(1,128)}, f32[1,1]{1,0:T(1,128)}) fusion(f32[8,128]{1,0:T(8,128)S(1)} %get-tuple-element.5), kind=kLoop, calls=%fused_computation.2 | loop fusion | bytes 16 | tf_op jit(solution)/shard_map/slice | solution.py:496
  44.4 2.8 %multiply_add_fusion = (f32[1024,256]{1,0:T(8,128)}, f32[1024,256]{1,0:T(8,128)}) fusion(f32[1024,256]{1,0:T(8,128)S(1)} %get-tuple-element.7, f32[1024,256]{1,0:T(8,128)S(1)} %copy-done, f32[1024,256]{1,0:T(8,128)S(1)} %get-tuple-element.6, f32[]{:T(128)} %bitcast.1, f32[]{:T(128)} %bitcast), kind=kLoop, calls=%fused_computation | loop fusion | flops 1835008 | bytes 5242888 | tf_op jit(solution)/shard_map/add | solution.py:498
Async XLA Ops:
  0.6 1.2 %copy-start = (f32[1024,256]{1,0:T(8,128)S(1)}, f32[1024,256]{1,0:T(8,128)}, u32[]{:S(2)}) copy-start(f32[1024,256]{1,0:T(8,128)} %right_ref.1) | copy-start | bytes 3145732
  1.9 1.4 %copy-start.1 = (s32[24,128,128]{2,1,0:T(8,128)S(1)}, s32[24,128,128]{2,1,0:T(8,128)}, u32[]{:S(2)}) copy-start(s32[24,128,128]{2,1,0:T(8,128)} %mask_ref.1) | copy-start | bytes 4718596
  3.3 1.0 %copy-start.2 = (f32[1024,128]{1,0:T(8,128)S(1)}, f32[1024,128]{1,0:T(8,128)}, u32[]{:S(2)}) copy-start(f32[1024,128]{1,0:T(8,128)} %self_ref.1) | copy-start | bytes 1572868
  4.3 1.0 %copy-start.3 = (f32[1024,128]{1,0:T(8,128)S(1)}, f32[1024,128]{1,0:T(8,128)}, u32[]{:S(2)}) copy-start(f32[1024,128]{1,0:T(8,128)} %next_ref.1) | copy-start | bytes 1572868
  5.4 0.9 %copy-start.4 = (f32[256,256]{1,0:T(8,128)S(1)}, f32[256,256]{1,0:T(8,128)}, u32[]{:S(2)}) copy-start(f32[256,256]{1,0:T(8,128)} %panel_ref.1) | copy-start | bytes 786436
  6.3 0.7 %copy-start.5 = (s32[24]{0:T(128)S(1)}, s32[24]{0:T(128)}, u32[]{:S(2)}) copy-start(s32[24]{0:T(128)} %users_ref.1) | copy-start | bytes 292
  7.0 0.7 %copy-start.6 = (s32[24]{0:T(128)S(1)}, s32[24]{0:T(128)}, u32[]{:S(2)}) copy-start(s32[24]{0:T(128)} %items_ref.1) | copy-start | bytes 292

commit v2 on v1

--- a/solution.py
+++ b/solution.py
@@ -61,10 +61,9 @@
     w_lo,
     diag,
     ahead,
-    carried,
-    product,
-    columns_out,
-    columns_in,
+    behind,
+    edge_out,
+    next_in,
     mine,
     near,
     near_sum,
@@ -81,16 +80,16 @@
     far_s,
     far_r,
 ):
-    R, L, g, T, U, K, PR, per_panel = sizes
-    Z = R // g
-    G = g * L
+    R, L, g, gr, T, U, K, PR, per_panel = sizes
+    Z = R // gr
+    G = gr * L
     row, loop = lax.axis_index("row"), lax.axis_index("loop")
     n = R * L
     d = row * L + loop
-    me_near = lax.rem(row, g) * L + loop
-    me_far = row // g
+    me_near = lax.rem(row, gr) * L + loop
+    me_far = row // gr
     quarter = lax.rem(row, g)
-    base = me_far * g
+    base = row // g * g
     after, before = lax.rem(d + 1, n), lax.rem(d + n - 1, n)
     after = (after // L, lax.rem(after, L))
     before = (before // L, lax.rem(before, L))
@@ -114,11 +113,11 @@
 
     def near_device(i):
         t = lax.rem(me_near + i, G)
-        return t, (base + t // L, lax.rem(t, L))
+        return t, (me_far * gr + t // L, lax.rem(t, L))
 
     def far_device(i):
         t = lax.rem(me_far + i, Z)
-        return t, (t * g + quarter, loop)
+        return t, (t * gr + lax.rem(row, gr), loop)
 
     barrier = pltpu.get_barrier_semaphore()
     greeted = [near_device(i)[1] for i in range(1, G)] + [far_device(i)[1] for i in range(1, Z)]
@@ -158,21 +157,29 @@
         t = lax.rem(quarter + i, g)
         return remote(share(k, t), share(k, t), share_s.at[k, i], share_r.at[k, t], (base + t, loop))
 
-    first_0 = remote(right_ref.at[pl.ds(0, T)], ahead.at[0], halo_s.at[0, 0], halo_r.at[0, 0], before)
-    first_1 = remote(q_v.at[pl.ds(0, T)], ahead.at[1], halo_s.at[1, 0], halo_r.at[1, 0], before)
-    product_copies = [
-        remote(product.at[ph], carried.at[ph], halo_s.at[ph, 1], halo_r.at[ph, 1], after) for ph in range(2)
+    to_before = [
+        remote(src, ahead.at[ph], halo_s.at[ph, 0], halo_r.at[ph, 0], before)
+        for ph, src in enumerate([right_ref.at[pl.ds(0, T)], edge_out.at[0]])
     ]
-    columns_copy = remote(columns_out, columns_in, halo_s.at[0, 2], halo_r.at[0, 2], after)
+    to_after = [
+        remote(src, behind.at[ph], halo_s.at[ph, 1], halo_r.at[ph, 1], after)
+        for ph, src in enumerate([right_ref.at[pl.ds(tail, T)], edge_out.at[1]])
+    ]
+    tile_copy = remote(next_ref.at[pl.ds(tail, T)], next_in, halo_s.at[0, 2], halo_r.at[0, 2], after)
 
     @pl.when(has_before)
     def _():
-        first_0.start()
+        to_before[0].start()
 
     @pl.when(jnp.logical_not(has_before))
     def _():
-        carried[...] = jnp.zeros_like(carried)
-        columns_in[...] = jnp.zeros_like(columns_in)
+        behind[...] = jnp.zeros_like(behind)
+        next_in[...] = jnp.zeros_like(next_in)
+
+    @pl.when(has_after)
+    def _():
+        tile_copy.start()
+        to_after[0].start()
 
     @pl.when(jnp.logical_not(has_after))
     def _():
@@ -180,15 +187,6 @@
 
     loads[0].wait()
     loads[1].wait()
-    last_next = next_v[tail:]
-    columns_out[...] = jnp.broadcast_to(jnp.sum(last_next, axis=0, keepdims=True), columns_out.shape)
-    last_turned = halves(last_next.T)
-    product[0] = dot3(last_turned, halves(b_v[tail:]), NN)
-
-    @pl.when(has_after)
-    def _():
-        columns_copy.start()
-        product_copies[0].start()
 
     loads[2].wait()
     degrees = []
@@ -254,17 +252,18 @@
         return dot3(halves(scores), panel, NN)
 
     split_field(b_v)
-    pairs = [(0, 1)] + [(U - 2, U - 1)] + [(b, b + 1) for b in range(2, U - 2, 2)]
-
-    for b in range(U):
-        q_v[b * T : (b + 1) * T] = inner(b, b_v)
-
     passed = []
     for k in range(1, L):
         direct[k - 1].wait_recv()
-        passed += forwards(k)
-        for copy in passed[-(g - 1) :] if g > 1 else []:
+        sent = forwards(k)
+        for copy in sent:
             copy.start()
+        passed += sent
+
+    pairs = [(0, 1)] + [(U - 2, U - 1)] + [(b, b + 1) for b in range(2, U - 2, 2)]
+
+    for b in range(U):
+        q_v[b * T : (b + 1) * T] = inner(b, b_v)
 
     loads[3].wait()
     split_panel(0)
@@ -286,38 +285,16 @@
         for k in range(1, L):
             add_gram(k, blocks, q_v)
 
-    def edges(ph, out):
-        @pl.when(has_before)
-        def _():
-            product_copies[ph].wait_recv()
-
-        out[:T] = out[:T] - carried[ph]
-
-        @pl.when(has_after)
-        def _():
-            (first_0, first_1)[ph].wait_recv()
-
-        tile = (w_hi[U - 1, :, 2 * T :], w_lo[U - 1, :, 2 * T :])
-        out[tail:] = out[tail:] - dot3(tile, halves(ahead[ph]), NN)
+    edge_out[0] = q_v[:T]
+    edge_out[1] = q_v[tail:]
 
     @pl.when(has_before)
     def _():
-        columns_copy.wait_recv()
-
-    entering = jnp.broadcast_to(columns_in[:1], (T, T)).T
-    diag[:T] = diag[:T] + entering
-    q_v[:T] = q_v[:T] + jnp.concatenate([entering] * (K // T), axis=1) * b_v[:T]
-    edges(0, q_v)
-
-    @pl.when(has_before)
-    def _():
-        first_1.start()
-
-    product[1] = dot3(last_turned, halves(q_v[tail:]), NN)
+        to_before[1].start()
 
     @pl.when(has_after)
     def _():
-        product_copies[1].start()
+        to_after[1].start()
 
     for blocks in pairs[2:]:
         for k in range(1, L):
@@ -358,57 +335,90 @@
             total = total + far[ph, lax.rem(me_far + i, Z)]
         return jnp.sum(total, axis=1, keepdims=True)
 
-    norm = jnp.zeros((1, 128), F32)
-    energy = jnp.zeros((1, 128), F32)
-    for b in range(U):
-        rows = slice(b * T, (b + 1) * T)
-        norm = norm + lanes(b_v[rows] * b_v[rows])
-        energy = energy + lanes(b_v[rows] * q_v[rows])
-    store_sums(0, [norm, energy])
-    start_near(0)
+    @pl.when(has_before)
+    def _():
+        tile_copy.wait_recv()
+        to_after[0].wait_recv()
+
+    @pl.when(has_after)
+    def _():
+        to_before[0].wait_recv()
+
+    def wide(column):
+        return jnp.concatenate([column] * (K // T), axis=1)
+
+    def spread_columns(tile):
+        return jnp.broadcast_to(jnp.sum(tile.T, axis=1, keepdims=True), (T, T))
+
+    entering_tile = next_in[...]
+    entering = halves(entering_tile)
+    turned_in = halves(entering_tile.T)
+    last_next = next_v[tail:]
+    leaving = halves(last_next)
+    turned_out = halves(last_next.T)
+    columns = spread_columns(entering_tile)
+    diag[:T] = diag[:T] + columns
+    q_v[:T] = q_v[:T] + wide(columns) * b_v[:T] - dot3(turned_in, halves(behind[0]), NN)
+    q_v[tail:] = q_v[tail:] - dot3(leaving, halves(ahead[0]), NN)
+    behind_more = dot3(entering, (v_hi[:T], v_lo[:T]), NN)
+    ahead_more = wide(spread_columns(last_next)) * ahead[0] - dot3(turned_out, (v_hi[tail:], v_lo[tail:]), NN)
     q_copy = pltpu.make_async_copy(q_v, q_out, local_sem.at[5])
     q_copy.start()
 
     split_field(q_v)
     for b in range(U):
         p_v[b * T : (b + 1) * T] = inner(b, q_v)
-    for blocks in pairs:
-        add_gram(0, blocks, p_v)
+    for k in range(L):
+        for blocks in pairs:
+            add_gram(k, blocks, p_v)
+
+    totals = [jnp.zeros((1, 128), F32)] * 4
+    edge_blocks = (0, U - 1)
+
+    def add_sum(at, left, right, b):
+        rows = slice(b * T, (b + 1) * T)
+        totals[at] = totals[at] + lanes(left[rows] * right[rows])
+
+    for b in range(U):
+        add_sum(0, b_v, b_v, b)
+        add_sum(1, b_v, q_v, b)
+        add_sum(2, q_v, q_v, b)
+        if b not in edge_blocks:
+            add_sum(3, q_v, p_v, b)
+
+    @pl.when(has_before)
+    def _():
+        to_after[1].wait_recv()
+
+    @pl.when(has_after)
+    def _():
+        to_before[1].wait_recv()
+
+    coupled_after = jnp.where(has_after, F32(1), F32(0))
+    p_v[:T] = p_v[:T] - dot3(turned_in, halves(behind[1] - behind_more), NN)
+    p_v[tail:] = p_v[tail:] - dot3(leaving, halves(coupled_after * (ahead[1] + ahead_more)), NN)
+    for b in edge_blocks:
+        add_sum(3, q_v, p_v, b)
+    p_copy = pltpu.make_async_copy(p_v, p_out, local_sem.at[6])
+    store_sums(0, totals)
+    start_near(0)
+    p_copy.start()
     near_to_far(0)
-    for blocks in pairs:
-        for k in range(1, L):
-            add_gram(k, blocks, p_v)
-    edges(1, p_v)
-    p_copy = pltpu.make_async_copy(p_v, p_out, local_sem.at[6])
-    p_copy.start()
-
     sums = finish_far(0)
-    norm_0, energy_0 = sums[0:1], sums[1:2]
+    norm_0, energy_0, square, energy_q = sums[0:1], sums[1:2], sums[2:3], sums[3:4]
     step_0 = norm_0 / energy_0
-    norm = jnp.zeros((1, 128), F32)
-    energy = jnp.zeros((1, 128), F32)
-    cross = jnp.zeros((1, 128), F32)
-    for b in range(U):
-        rows = slice(b * T, (b + 1) * T)
-        image = q_v[rows]
-        residual = b_v[rows] - step_0 * image
-        norm = norm + lanes(residual * residual)
-        energy = energy + lanes(residual * (image - step_0 * p_v[rows]))
-        cross = cross + lanes(residual * image)
-    store_sums(1, [norm, energy, cross])
-    start_near(1)
-    near_to_far(1)
-    sums = finish_far(1)
-    norm_1, energy_1, cross_1 = sums[0:1], sums[1:2], sums[2:3]
+    norm_1 = norm_0 - 2.0 * step_0 * energy_0 + step_0 * step_0 * square
     beta = norm_1 / norm_0
-    step_1 = norm_1 / (energy_1 + 2.0 * beta * cross_1 + beta * beta * energy_0)
-    first = step_0 + step_1 * (1.0 + beta)
+    more = 1.0 + beta
+    energy_1 = more * (more * energy_0 - 2.0 * step_0 * square) + step_0 * step_0 * energy_q
+    step_1 = norm_1 / energy_1
+    first = step_0 + step_1 * more
     second = step_0 * step_1
     coef_out[...] = jnp.concatenate([jnp.broadcast_to(first, (4, 128)), jnp.broadcast_to(second, (4, 128))], axis=0)
 
     for copy in direct + passed:
         copy.wait_send()
-    for ph in range(2):
+    for ph in (0,):
         for i in range(1, G):
             near_copy(ph, i, True).wait_send()
         for i in range(1, Z):
@@ -416,23 +426,31 @@
 
     @pl.when(has_before)
     def _():
-        first_0.wait_send()
-        first_1.wait_send()
+        for copy in to_before:
+            copy.wait_send()
 
     @pl.when(has_after)
     def _():
-        columns_copy.wait_send()
-        for copy in product_copies:
+        tile_copy.wait_send()
+        for copy in to_after:
             copy.wait_send()
 
     q_copy.wait()
     p_copy.wait()
+
+
+def finish(coef_ref, right_ref, q_ref, p_ref, solution_ref, residual_ref):
+    first, second = coef_ref[0:1, 0:1], coef_ref[4:5, 0:1]
+    right, q = right_ref[...], q_ref[...]
+    solution_ref[...] = first * right - second * q
+    residual_ref[...] = right - first * q + second * p_ref[...]
 
 
 def body(panels, right_side, block_users, block_items, masks, self_tiles, next_tiles):
     R, L = lax.axis_size("row"), lax.axis_size("loop")
     g = 4 if R % 4 == 0 else R
-    Z, G = R // g, 4 * L if R % 4 == 0 else R * L
+    gr = g
+    Z, G = R // gr, gr * L
     T = masks.shape[1]
     PR, K = panels.shape
     rows = right_side.shape[0]
@@ -440,7 +458,7 @@
     entries = masks.shape[0]
     per_panel = entries // L
     assert per_panel < 1 << COUNT_BITS and U * COUNT_BITS <= 32
-    sizes = (R, L, g, T, U, K, PR, per_panel)
+    sizes = (R, L, g, gr, T, U, K, PR, per_panel)
     hbm = pl.BlockSpec(memory_space=pl.ANY)
     smem = pl.BlockSpec(memory_space=pltpu.SMEM)
     vmem = pl.BlockSpec(memory_space=pltpu.VMEM)
@@ -470,12 +488,11 @@
             pltpu.VMEM((2, T, K), F32),
             pltpu.VMEM((2, T, K), F32),
             pltpu.VMEM((2, T, K), F32),
-            pltpu.VMEM((8, T), F32),
-            pltpu.VMEM((8, T), F32),
-            pltpu.VMEM((2, 8, 128), F32),
-            pltpu.VMEM((2, G, 8, 128), F32),
-            pltpu.VMEM((2, 8, 128), F32),
-            pltpu.VMEM((2, Z, 8, 128), F32),
+            pltpu.VMEM((T, T), F32),
+            pltpu.VMEM((1, 8, 128), F32),
+            pltpu.VMEM((1, G, 8, 128), F32),
+            pltpu.VMEM((1, 8, 128), F32),
+            pltpu.VMEM((1, Z, 8, 128), F32),
             dma((7,)),
             dma((L,)),
             dma((L,)),
@@ -483,20 +500,25 @@
             dma((L, g)),
             dma((2, 3)),
             dma((2, 3)),
-            dma((2, G)),
-            dma((2, G)),
-            dma((2, Z)),
-            dma((2, Z)),
+            dma((1, G)),
+            dma((1, G)),
+            dma((1, Z)),
+            dma((1, Z)),
         ],
         compiler_params=pltpu.CompilerParams(
-            collective_id=0, has_side_effects=True, vmem_limit_bytes=32 * 1024 * 1024
+            collective_id=0, has_side_effects=True, vmem_limit_bytes=60 * 1024 * 1024
         ),
         cost_estimate=pl.CostEstimate(flops=8 * rows * K * PR * L, bytes_accessed=8 * rows * K * 4, transcendentals=0),
     )(block_users, block_items, panels, right_side, masks, self_tiles, next_tiles)
-    first, second = coef[0, 0], coef[4, 0]
-    solution_field = first * right_side - second * q
-    residual = right_side - first * q + second * p
-    return solution_field, residual
+    steps = 4
+    block = pl.BlockSpec((rows // steps, K), lambda i: (i, 0))
+    return pl.pallas_call(
+        finish,
+        grid=(steps,),
+        out_shape=(field, field),
+        in_specs=[pl.BlockSpec((8, 128), lambda i: (0, 0)), block, block, block],
+        out_specs=(block, block),
+    )(coef, right_side, q, p)
 
 
 def solution(mesh):

time: 47.6 us -> 35.9 us (0.75)
  local copies, waits for them, and re-layouts: 7.53 us -> 0 us
  other arithmetic: 2.82 us -> 0 us
  Pallas kernels: 36.2 us -> 35.1 us
    unnamed x14 -> x0, local copies, waits for them, and re-layouts: 6.97 us -> none
    pallas_call x1, Pallas kernels: 36.2 us -> 31 us  [body(): pl.pallas_call(functools.partial(kernel, sizes), out_shape=(field, field,...]
    pallas_call x0 -> x1, Pallas kernels: none -> 4.06 us  [body(): pl.pallas_call(finish, grid=(steps,), out_shape=(field, field), in_specs=...]
    add x1 -> x0, other arithmetic: 2.82 us -> none  [body(): residual = right_side - first * q + second * p]
    slice x1 -> x0, local copies, waits for them, and re-layouts: 0.57 us -> none  [body(): first, second = (coef[0, 0], coef[4, 0])]
where the time goes in v2:
time: 35.9 us; the launch traced here: 35.7 us
  Pallas kernels  35.1 us (98%)
  between operations  0.64 us (2%)
    pallas_call x1, Pallas kernels, body(): pl.pallas_call(functools.partial(kernel, sizes), out_shape=(field, field,...  31 us
    pallas_call x1, Pallas kernels, body(): pl.pallas_call(finish, grid=(steps,), out_shape=(field, field), in_specs=...  4.06 us

profile of v2, /device:TPU:0, one launch (start us, length us, event | category | flops | bytes accessed | tf_op | source)
XLA Modules:
  0.0 35.7 jit_solution(17057439546731357391)
XLA Ops:
  0.6 31.0 %shard_map.86 = (f32[1024,256]{1,0:T(8,128)}, f32[1024,256]{1,0:T(8,128)}, f32[8,128]{1,0:T(8,128)}) custom-call(s32[24]{0:T(128)} %users_ref.1, s32[24]{0:T(128)} %items_ref.1, f32[256,256]{1,0:T(8,128)} %panel_ref.1, f32[1024,256]{1,0:T(8,128)} %right_ref.3, s32[24,128,128]{2,1,0:T(8,128)} %mask_ref.1, f32[1024,128]{1,0:T(8,128)} %self_ref.1, ...), custom_call_target="tpu_custom_call" | custom-call | flops 1073741824 | bytes 8388608 | tf_op jit(solution)/shard_map/pallas_call | solution.py:467
  31.7 4.1 %shard_map.87 = (f32[1024,256]{1,0:T(8,128)}, f32[1024,256]{1,0:T(8,128)}) custom-call(f32[8,128]{1,0:T(8,128)} %get-tuple-element.5.coef_ref, f32[1024,256]{1,0:T(8,128)} %right_ref.3, f32[1024,256]{1,0:T(8,128)} %get-tuple-element.6.q_ref, f32[1024,256]{1,0:T(8,128)} %get-tuple-element.7.p_ref), custom_call_target="tpu_custom_call" | custom-call | tf_op jit(solution)/shard_map/pallas_call | solution.py:515

commit v3 on v2

--- a/solution.py
+++ b/solution.py
@@ -510,7 +510,7 @@
         ),
         cost_estimate=pl.CostEstimate(flops=8 * rows * K * PR * L, bytes_accessed=8 * rows * K * 4, transcendentals=0),
     )(block_users, block_items, panels, right_side, masks, self_tiles, next_tiles)
-    steps = 4
+    steps = 2
     block = pl.BlockSpec((rows // steps, K), lambda i: (i, 0))
     return pl.pallas_call(
         finish,

time: 35.9 us -> 34.9 us (0.972)
  Pallas kernels: 35.1 us -> 34 us
    pallas_call x1, Pallas kernels: 4.06 us -> 3 us  [body(): pl.pallas_call(finish, grid=(steps,), out_shape=(field, field), in_specs=...]
where the time goes in v3:
time: 34.9 us; the launch traced here: 34.7 us
  Pallas kernels  34 us (97%)
  between operations  0.64 us (2%)
    pallas_call x1, Pallas kernels, body(): pl.pallas_call(functools.partial(kernel, sizes), out_shape=(field, field,...  31 us
    pallas_call x1, Pallas kernels, body(): pl.pallas_call(finish, grid=(steps,), out_shape=(field, field), in_specs=...  3 us

profile of v3, /device:TPU:0, one launch (start us, length us, event | category | flops | bytes accessed | tf_op | source)
XLA Modules:
  0.0 34.7 jit_solution(1775041250756901165)
XLA Ops:
  0.6 31.0 %shard_map.86 = (f32[1024,256]{1,0:T(8,128)}, f32[1024,256]{1,0:T(8,128)}, f32[8,128]{1,0:T(8,128)}) custom-call(s32[24]{0:T(128)} %users_ref.1, s32[24]{0:T(128)} %items_ref.1, f32[256,256]{1,0:T(8,128)} %panel_ref.1, f32[1024,256]{1,0:T(8,128)} %right_ref.3, s32[24,128,128]{2,1,0:T(8,128)} %mask_ref.1, f32[1024,128]{1,0:T(8,128)} %self_ref.1, ...), custom_call_target="tpu_custom_call" | custom-call | flops 1073741824 | bytes 8388608 | tf_op jit(solution)/shard_map/pallas_call | solution.py:467
  31.7 3.0 %shard_map.87 = (f32[1024,256]{1,0:T(8,128)}, f32[1024,256]{1,0:T(8,128)}) custom-call(f32[8,128]{1,0:T(8,128)} %get-tuple-element.5.coef_ref, f32[1024,256]{1,0:T(8,128)} %right_ref.3, f32[1024,256]{1,0:T(8,128)} %get-tuple-element.6.q_ref, f32[1024,256]{1,0:T(8,128)} %get-tuple-element.7.p_ref), custom_call_target="tpu_custom_call" | custom-call | tf_op jit(solution)/shard_map/pallas_call | solution.py:515
